TPU v7x, 32 devices: a whole 2x2x4 slice. The times are simulated.
32 devices in a mesh: slab: 8 (over y, x, core), view: 4 (over z).
Axes of the slice: x: 2, y: 2, z: 4, core: 2. Of those that a mesh axis runs over, the one named last changes fastest.
Arguments:
- volume: float32 [8, 64, 4096], P('view', 'slab'), may hold values from -6 to 6
- vox_inv: float32 [8, 64, 4096], P('view', 'slab'), may hold values from 0.01 to 0.1
- measured: float32 [128, 12, 4096], P('slab', 'view'), may hold values from -24 to 24
- ray_inv: float32 [128, 12, 4096], P('slab', 'view'), may hold values from 0.05 to 0.5
- col_shift: int32 [12, 8], replicated, may hold values from -512 to 512
- col_frac: float32 [12, 8], replicated, may hold values from 0 to 1
- row_offset: int32 [12, 64], P('view', 'slab'), may hold values from -8 to 8, as said below
- row_frac: float32 [12, 64], P('view', 'slab'), may hold values from 0 to 1
Outputs:
- updated: float32 [8, 64, 4096], P('view', 'slab')
- residual: bfloat16 [128, 12, 4096], P('slab', 'view')
Inputs may be any that keep to these rules, and one draw needn't show every extreme that they name: `row_offset`: every entry lies in -8 to 8, and both ends occur.
All inputs are finite; a program needn't handle non-finite values.
Results may differ from a plain program's by a relative error of at most 0.0095.
Values may be sent and summed in bfloat16 or wider, within the bound.
A program may use at most 64 MiB of HBM per device.

v0:
```python
import jax
import jax.numpy as jnp
from jax import lax
from jax.sharding import PartitionSpec as P


def from_behind(x, axis, by):
    devices = lax.axis_size(axis)
    pairs = [(i, i + by) for i in range(devices) if 0 <= i + by < devices]
    return lax.ppermute(x, axis, pairs)


def with_halo(block, sides, width):
    for axis, dim in sides:
        count = lax.axis_size(axis)
        forward = [(i, i + 1) for i in range(count - 1)]
        backward = [(target, source) for source, target in forward]
        low = lax.ppermute(
            lax.slice_in_dim(block, block.shape[dim] - width, None, axis=dim), axis, forward
        )
        high = lax.ppermute(lax.slice_in_dim(block, 0, width, axis=dim), axis, backward)
        block = jnp.concatenate([low, block, high], axis=dim)
    return block


def band_rows(base, frac, rows):
    r = rows[None, :, None]
    first = jnp.where(r == base[:, None, :], 1.0 - frac[:, None, :], 0.0)
    second = jnp.where(r == base[:, None, :] + 1, frac[:, None, :], 0.0)
    return first + second


def pad_columns(block):
    width = block.shape[-1]
    margin = width // 8 + 1
    widths = [(0, 0)] * (block.ndim - 1) + [(margin, margin)]
    return (jnp.pad(block, widths), margin)


def shear_forward(padded, margin, width, shift, frac):
    count = padded.shape[0]
    total = jnp.zeros((padded.shape[1], width), jnp.float32)
    for line in range(count):
        start = shift[line] + margin
        taps_a = lax.dynamic_slice_in_dim(padded[line], start, width, 1).astype(jnp.float32)
        taps_b = lax.dynamic_slice_in_dim(padded[line], start + 1, width, 1).astype(jnp.float32)
        total = total + (1.0 - frac[line]) * taps_a + frac[line] * taps_b
    return total


def shear_back(padded, margin, width, shift, frac):
    count = shift.shape[0]
    results = []
    for line in range(count):
        start = margin - shift[line]
        taps_a = lax.dynamic_slice_in_dim(padded, start, width, 1).astype(jnp.float32)
        taps_b = lax.dynamic_slice_in_dim(padded, start - 1, width, 1).astype(jnp.float32)
        results.append((1.0 - frac[line]) * taps_a + frac[line] * taps_b)
    return jnp.stack(results)


def per_device(volume, vox_inv, measured, ray_inv, col_shift, col_frac, row_offset, row_frac):
    y_dev, z_dev, width = volume.shape
    row_dev, view_dev = (measured.shape[0], measured.shape[1])
    slab_at = lax.axis_index("slab")
    view_at = lax.axis_index("view")
    own_shift = lax.dynamic_slice_in_dim(col_shift, view_at * view_dev, view_dev, 0)
    own_frac = lax.dynamic_slice_in_dim(col_frac, view_at * view_dev, view_dev, 0)
    z_global = slab_at * z_dev + jnp.arange(z_dev, dtype=jnp.int32)
    base = z_global[None, :] * row_dev // z_dev + row_offset
    lines = volume.astype(jnp.bfloat16)
    piece = lax.all_gather(lines, "view", axis=0, tiled=True)
    padded, add_margin = pad_columns(piece)
    images_now = []
    for view in range(view_dev):
        shift = own_shift[view]
        frac = own_frac[view]
        images_now.append(shear_forward(padded, add_margin, width, shift, frac))
    sheared = jnp.stack(images_now)
    rows = (slab_at - 1) * row_dev + jnp.arange(3 * row_dev, dtype=jnp.int32)
    band = band_rows(base, row_frac, rows)
    local = jnp.einsum("vrz,vzc->rvc", band, sheared, precision=lax.Precision.HIGHEST)
    local = lax.optimization_barrier(local.astype(jnp.bfloat16))
    from_below = from_behind(local[2 * row_dev :], "slab", 1)
    from_above = from_behind(local[:row_dev], "slab", -1)
    projected = (
        local[row_dev : 2 * row_dev].astype(jnp.float32)
        + from_below.astype(jnp.float32)
        + from_above.astype(jnp.float32)
    )
    residual = (ray_inv * (measured - projected)).astype(jnp.bfloat16)
    rim = with_halo(residual, (("slab", 0),), row_dev)
    images = jnp.einsum(
        "vrz,rvc->vzc", band, rim.astype(jnp.float32), precision=lax.Precision.HIGHEST
    )
    images = images.astype(jnp.bfloat16)
    padded_images, margin = pad_columns(images)
    total = jnp.zeros((y_dev * lax.axis_size("view"), z_dev, width), jnp.float32)
    for view in range(view_dev):
        shift = own_shift[view]
        frac = own_frac[view]
        total = total + shear_back(padded_images[view], margin, width, shift, frac)
    back = lax.psum_scatter(
        total.astype(jnp.bfloat16), "view", scatter_dimension=0, tiled=True
    ).astype(jnp.float32)
    updated = volume + vox_inv * back
    return (updated, residual)


def solution(mesh):
    in_specs = (
        P("view", "slab", None),
        P("view", "slab", None),
        P("slab", "view", None),
        P("slab", "view", None),
        P(),
        P(),
        P("view", "slab"),
        P("view", "slab"),
    )
    out_specs = (P("view", "slab", None), P("slab", "view", None))
    return jax.shard_map(
        per_device, mesh=mesh, in_specs=in_specs, out_specs=out_specs, check_vma=False
    )
```

profile of v0, /device:TPU:0, one launch (start us, length us, event | category | flops | bytes accessed | tf_op | source)
XLA Modules:
  0.0 253.2 jit_solution(10525530276075594291)
XLA Ops:
  7.2 0.0 copy-start
  7.2 0.0 reduce-scatter.2.cloned.1.call-start
  7.2 0.6 copy-done
  7.9 0.1 constant_dynamic-slice_fusion
  7.9 0.7 fusion.33
  53.5 0.6 fusion.35
  55.2 0.8 constant_dynamic-slice_fusion.1
  56.0 0.7 fusion.32
  56.7 0.6 fusion.34
  70.8 1.0 convert_element_type.419
  71.7 0.0 copy-start.6
  71.7 0.0 copy-start.7
  71.8 17.4 %all_gather.3 = bf16[8,8,4096]{2,1,0:T(8,128)(2,1)S(1)} all-gather(bf16[2,8,4096]{2,1,0:T(8,128)(2,1)S(1)} %convert_element_type.419), channel_id=1, replica_groups=mesh['slab'=8,'view'=4] {'view'}, dimensions={0}, use_global_device_ids=true | all-gather | bytes 655360 | tf_op jit(solution)/shard_map/all_gather | solution.py:72
  89.1 0.2 pad_slice_fusion.7
  105.1 5.6 %multiply_add_fusion.1 = f32[1,8,4096]{2,1,0:T(8,128)S(1)} fusion(bf16[1,8,5122]{2,1,0:T(8,128)(2,1)S(1)} %get-tuple-element.13, s32[]{:T(128)S(6)} %select_n.360, f32[]{:T(128)} %bitcast.115, s32[]{:T(128)S(6)} %select_n.359, f32[]{:T(128)S(6)} %sub.400, bf16[1,8,5122]{2,1,0:T(8,128)(2,1)S(1)} %get-tuple-element.12, s32[]{:T(128)S(6)} %select_n.358, ...), kind=kLoop, calls=%fused_computation.51 | loop fusion | flops 1540096 | bytes 1179776 | tf_op jit(solution)/shard_map/add | solution.py:47
  110.7 5.5 %multiply_add_fusion.2 = f32[1,8,4096]{2,1,0:T(8,128)S(1)} fusion(bf16[1,8,5122]{2,1,0:T(8,128)(2,1)S(1)} %get-tuple-element.13, s32[]{:T(128)S(6)} %select_n.344, f32[]{:T(128)} %bitcast.75, s32[]{:T(128)S(6)} %select_n.343, f32[]{:T(128)S(6)} %sub.392, bf16[1,8,5122]{2,1,0:T(8,128)(2,1)S(1)} %get-tuple-element.12, s32[]{:T(128)S(6)} %select_n.342, ...), kind=kLoop, calls=%fused_computation.52 | loop fusion | flops 1540096 | bytes 1179776 | tf_op jit(solution)/shard_map/add | solution.py:47
  116.2 5.6 %multiply_add_fusion.3 = f32[1,8,4096]{2,1,0:T(8,128)S(1)} fusion(bf16[1,8,5122]{2,1,0:T(8,128)(2,1)S(1)} %get-tuple-element.13, s32[]{:T(128)S(6)} %select_n.328, f32[]{:T(128)} %bitcast.35, s32[]{:T(128)S(6)} %select_n.327, f32[]{:T(128)S(6)} %sub.384, bf16[1,8,5122]{2,1,0:T(8,128)(2,1)S(1)} %get-tuple-element.12, s32[]{:T(128)S(6)} %select_n.326, ...), kind=kLoop, calls=%fused_computation.53 | loop fusion | flops 1540096 | bytes 1179776 | tf_op jit(solution)/shard_map/add | solution.py:47
  121.7 2.1 fusion
  123.8 0.0 copy-start.2
  123.9 0.0 copy-start.3
  123.9 0.1 fusion.31
  123.9 1.4 collective-permute-start.1
  125.4 3.1 %collective-permute-start = (bf16[16,3,4096]{2,0,1:T(8,128)(2,1)S(1)}, bf16[16,3,4096]{2,0,1:T(8,128)(2,1)S(1)}, u32[]{:S(2)}, u32[]{:S(2)}) collective-permute-start(bf16[16,3,4096]{2,0,1:T(8,128)(2,1)S(1)} %get-tuple-element.4), channel_id=1, source_target_pairs={{0,4},{4,8},{8,12},{12,16},{16,20},{20,24},{24,28},{1,5},{5,9},{9,... | collective-permute-start | bytes 1179656 | tf_op jit(solution)/shard_map/ppermute | solution.py:10
  128.4 0.0 collective-permute-done.1
  128.4 1.3 collective-permute-done
  129.7 0.2 multiply_convert_fusion
  129.9 0.0 copy-start.4
  130.0 1.3 collective-permute-start.3
  131.3 7.2 %collective-permute-start.2 = (bf16[16,3,4096]{2,0,1:T(8,128)(2,1)S(1)}, bf16[16,3,4096]{2,0,1:T(8,128)(2,1)S(1)}, u32[]{:S(2)}, u32[]{:S(2)}) collective-permute-start(bf16[16,3,4096]{2,0,1:T(8,128)(2,1)S(1)} %multiply_convert_fusion), channel_id=1, source_target_pairs={{0,4},{4,8},{8,12},{12,16},{16,20},{20,24},{24,28},{1,5},{5,9},{9,... | collective-permute-start | bytes 1179656 | tf_op jit(solution)/shard_map/ppermute | solution.py:18
  198.4 0.0 collective-permute-done.3
  198.4 0.0 collective-permute-done.2
  198.4 0.6 convolution_convert_fusion.1
  199.0 0.0 copy-done.4
  199.0 0.1 pad_slice_fusion.9
  199.2 0.7 add_dynamic-update-slice_fusion.7
  199.8 0.8 add_dynamic-update-slice_fusion.6
  200.7 0.7 add_dynamic-update-slice_fusion.5
  201.4 0.7 add_dynamic-update-slice_fusion.4
  202.1 0.8 add_dynamic-update-slice_fusion.3
  202.9 0.8 add_dynamic-update-slice_fusion.2
  203.7 0.7 add_dynamic-update-slice_fusion.1
  204.4 0.7 add_dynamic-update-slice_fusion.15
  205.1 0.7 add_dynamic-update-slice_fusion.14
  205.8 0.8 add_dynamic-update-slice_fusion.13
  206.6 0.8 add_dynamic-update-slice_fusion.12
  207.4 0.7 add_dynamic-update-slice_fusion.11
  208.1 0.7 add_dynamic-update-slice_fusion.10
  208.8 0.7 add_dynamic-update-slice_fusion.9
  209.5 0.8 add_dynamic-update-slice_fusion.23
  210.3 0.7 add_dynamic-update-slice_fusion.22
  211.1 0.7 add_dynamic-update-slice_fusion.21
  211.8 0.7 add_dynamic-update-slice_fusion.20
  212.6 0.7 add_dynamic-update-slice_fusion.19
  213.3 0.7 add_dynamic-update-slice_fusion.18
  214.0 0.7 add_dynamic-update-slice_fusion.17
  214.7 0.7 add_dynamic-update-slice_fusion.16
  215.5 1.4 add_dynamic-update-slice_fusion
  216.9 0.0 copy-start.1
  216.9 0.0 copy-start.5
  216.9 0.9 add_convert_fusion
  217.9 0.0 reduce-scatter.2.cloned.1.call-update
  217.9 26.8 %reduce-scatter.2.cloned.1.call-done = bf16[2,8,4096]{2,1,0:T(8,128)(2,1)} async-done(((bf16[8,8,4096]{2,1,0:T(8,128)(2,1)}), bf16[2,8,4096]{2,1,0:T(8,128)(2,1)}) %reduce-scatter.2.cloned.1.call-update) | async-done | bytes 131088 | tf_op jit(solution)/shard_map/reduce_scatter | solution.py:103
  244.7 0.0 copy-done.1
  244.7 1.6 multiply_add_fusion
  (9 shorter events, 0.0 us)
Async XLA Ops:
  7.2 0.7 copy-start
  7.2 237.5 %reduce-scatter.2.cloned.1.call-start = ((), (), s32[]{:S(2)}) async-start(), calls=%async_computation.1 | async-start | bytes 655360 | tf_op jit(solution)/shard_map/reduce_scatter | solution.py:103
  71.7 32.9 %copy-start.6 = (f32[3,8]{1,0:T(4,128)S(1)}, f32[3,8]{1,0:T(4,128)}, u32[]{:S(2)}) copy-start(f32[3,8]{1,0:T(4,128)} %param.15) | copy-start | bytes 292
  71.7 33.3 %copy-start.7 = (s32[3,8]{1,0:T(4,128)S(1)}, s32[3,8]{1,0:T(4,128)}, u32[]{:S(2)}) copy-start(s32[3,8]{1,0:T(4,128)} %param.14) | copy-start | bytes 292
  123.8 5.9 %copy-start.2 = (f32[16,3,4096]{2,0,1:T(8,128)S(1)}, f32[16,3,4096]{2,0,1:T(8,128)}, u32[]{:S(2)}) copy-start(f32[16,3,4096]{2,0,1:T(8,128)} %param.11) | copy-start | bytes 2359300
  123.9 5.9 %copy-start.3 = (f32[16,3,4096]{2,0,1:T(8,128)S(1)}, f32[16,3,4096]{2,0,1:T(8,128)}, u32[]{:S(2)}) copy-start(f32[16,3,4096]{2,0,1:T(8,128)} %param.10) | copy-start | bytes 2359300
  123.9 4.5 %collective-permute-start.1 = (bf16[16,3,4096]{2,0,1:T(8,128)(2,1)S(1)}, bf16[16,3,4096]{2,0,1:T(8,128)(2,1)S(1)}, u32[]{:S(2)}, u32[]{:S(2)}) collective-permute-start(bf16[16,3,4096]{2,0,1:T(8,128)(2,1)S(1)} %get-tuple-element.5), channel_id=1, source_target_pairs={{4,0},{8,4},{12,8},{16,12},{20,16},{24,20},{28,24},{5,1},{9,5},{13... | collective-permute-start | bytes 1179656 | tf_op jit(solution)/shard_map/ppermute | solution.py:10
  125.4 4.4 %collective-permute-start = (bf16[16,3,4096]{2,0,1:T(8,128)(2,1)S(1)}, bf16[16,3,4096]{2,0,1:T(8,128)(2,1)S(1)}, u32[]{:S(2)}, u32[]{:S(2)}) collective-permute-start(bf16[16,3,4096]{2,0,1:T(8,128)(2,1)S(1)} %get-tuple-element.4), channel_id=1, source_target_pairs={{0,4},{4,8},{8,12},{12,16},{16,20},{20,24},{24,28},{1,5},{5,9},{9,... | collective-permute-start | bytes 1179656 | tf_op jit(solution)/shard_map/ppermute | solution.py:10
  129.9 69.1 %copy-start.4 = (bf16[16,3,4096]{2,0,1:T(8,128)(2,1)}, bf16[16,3,4096]{2,0,1:T(8,128)(2,1)S(1)}, u32[]{:S(2)}) copy-start(bf16[16,3,4096]{2,0,1:T(8,128)(2,1)S(1)} %multiply_convert_fusion) | copy-start | bytes 1179652
  130.0 68.4 %collective-permute-start.3 = (bf16[16,3,4096]{2,0,1:T(8,128)(2,1)S(1)}, bf16[16,3,4096]{2,0,1:T(8,128)(2,1)S(1)}, u32[]{:S(2)}, u32[]{:S(2)}) collective-permute-start(bf16[16,3,4096]{2,0,1:T(8,128)(2,1)S(1)} %multiply_convert_fusion), channel_id=1, source_target_pairs={{4,0},{8,4},{12,8},{16,12},{20,16},{24,20},{28,24},{5,1},{9,5},{13... | collective-permute-start | bytes 1179656 | tf_op jit(solution)/shard_map/ppermute | solution.py:21
  131.3 67.1 %collective-permute-start.2 = (bf16[16,3,4096]{2,0,1:T(8,128)(2,1)S(1)}, bf16[16,3,4096]{2,0,1:T(8,128)(2,1)S(1)}, u32[]{:S(2)}, u32[]{:S(2)}) collective-permute-start(bf16[16,3,4096]{2,0,1:T(8,128)(2,1)S(1)} %multiply_convert_fusion), channel_id=1, source_target_pairs={{0,4},{4,8},{8,12},{12,16},{16,20},{20,24},{24,28},{1,5},{5,9},{9,... | collective-permute-start | bytes 1179656 | tf_op jit(solution)/shard_map/ppermute | solution.py:18
  216.9 27.8 %copy-start.1 = (f32[2,8,4096]{2,1,0:T(8,128)S(1)}, f32[2,8,4096]{2,1,0:T(8,128)}, u32[]{:S(2)}) copy-start(f32[2,8,4096]{2,1,0:T(8,128)} %param.8) | copy-start | bytes 786436
  216.9 27.8 %copy-start.5 = (f32[2,8,4096]{2,1,0:T(8,128)S(1)}, f32[2,8,4096]{2,1,0:T(8,128)}, u32[]{:S(2)}) copy-start(f32[2,8,4096]{2,1,0:T(8,128)} %param.9) | copy-start | bytes 786436
Sparse Core Ops, SparseCore 0:
  218.0 26.6 reduce-scatter.1
where the time goes:
time: 256 us; the launch traced here: 253 us
  between operations  149 us (58%)
  other arithmetic  38 us (15%)
  waiting for transfers between devices  28.2 us (11%)
  blocking collectives  17.4 us (7%)
  starting transfers between devices  13 us (5%)
  local copies, waits for them, and re-layouts  4.51 us (2%)
  matrix products  2.75 us (1%)
    reduce_scatter x1, waiting for transfers between devices, per_device(): lax.psum_scatter(total.astype(jnp.bfloat16), 'view', scatter_dimension=0,...  26.8 us
    all_gather x1, blocking collectives, per_device(): piece = lax.all_gather(lines, 'view', axis=0, tiled=True)  17.4 us
    add x3, other arithmetic, shear_forward(): total = total + (1.0 - frac[line]) * taps_a + frac[line] * taps_b  16.7 us
    unnamed x21, other arithmetic  15.4 us
    ppermute x1, starting transfers between devices, with_halo(): lax.ppermute(lax.slice_in_dim(block, block.shape[dim] - width, None, axis...  7.18 us
  transfers between devices with their start and end apart: 5, of which 2 were waited for; matrix products, arithmetic and copies ran while one was open for 0% of the time, Pallas kernels for 0%

commit v1 on v0

v1 whole, which is shorter than its diff:
```python
import functools

import jax
import jax.numpy as jnp
from jax import lax
from jax.experimental import pallas as pl
from jax.experimental.pallas import tpu as pltpu
from jax.sharding import PartitionSpec as P

F32 = jnp.float32
BF16 = jnp.bfloat16
LANES = 128


def dot(a, b):
    return jnp.dot(a, b, preferred_element_type=F32)


def kernel(
    sizes, vol, vox, meas, ray, shift, frac, off, rfrac, upd, res,
    gat, lines, taps_f, taps_b, acc, sheared, meta, resid, img_out, img_in, images, back_out, back_in,
    ag_send, ag_recv, me_send, me_recv, sh_send, sh_recv, im_send, im_recv, rs_send, rs_recv,
):
    n_view, n_slab, views, z_dev, row_dev, width = sizes
    half = width // 2
    margin = (lines.shape[1] * LANES - half) // 2
    blocks = half // LANES
    n_lines = 2 * n_view
    me = lax.axis_index("view")
    slab = lax.axis_index("slab")
    has_lo = slab > 0
    has_hi = slab < n_slab - 1

    def ag_copy(k):
        dest = lax.rem(me + k, n_view)
        return pltpu.make_async_remote_copy(
            gat.at[me], gat.at[me], ag_send.at[k], ag_recv.at[me], device_id={"view": dest}
        )

    def ag_arrival(src):
        return pltpu.make_async_remote_copy(
            gat.at[src], gat.at[src], ag_send.at[0], ag_recv.at[src], device_id={"view": src}
        )

    def rs_copy(k):
        dest = lax.rem(me + k, n_view)
        return pltpu.make_async_remote_copy(
            back_out.at[dest], back_in.at[me], rs_send.at[k], rs_recv.at[me], device_id={"view": dest}
        )

    def rs_arrival(src):
        return pltpu.make_async_remote_copy(
            back_out.at[src], back_in.at[src], rs_send.at[0], rs_recv.at[src], device_id={"view": src}
        )

    def halo(own, slots, send, recv, side, low_slot, high_slot):
        slot = high_slot if side == 0 else low_slot
        return pltpu.make_async_remote_copy(
            own, slots.at[slot], send.at[side], recv.at[1 - side],
            device_id={"slab": slab - 1 if side == 0 else slab + 1},
        )

    sides = ((0, has_lo), (1, has_hi))

    def meta_copy(side):
        return halo(meta.at[1], meta, me_send, me_recv, side, 0, 2)

    def sheared_copy(side):
        return halo(sheared.at[1], sheared, sh_send, sh_recv, side, 0, 2)

    def image_copy(side):
        return halo(img_out.at[side], img_in, im_send, im_recv, side, 0, 1)

    barrier = pltpu.get_barrier_semaphore()

    def greet(k, _):
        pl.semaphore_signal(barrier, inc=1, device_id={"view": lax.rem(me + k, n_view)})
        return 0

    lax.fori_loop(1, n_view, greet, 0)
    for side, has in sides:
        @pl.when(has)
        def _():
            pl.semaphore_signal(barrier, inc=1, device_id={"slab": slab - 1 if side == 0 else slab + 1})

    gat[me] = vol[...].reshape(2 * z_dev, width).astype(BF16)

    lane = lax.broadcasted_iota(jnp.int32, (8, LANES), 1)
    offs = jnp.zeros((8, LANES), F32)
    fracs = jnp.zeros((8, LANES), F32)
    for v in range(views):
        for z in range(z_dev):
            here = (lane // 16 == v) & (lane % 8 == z)
            offs = jnp.where(here, off[v, z].astype(F32), offs)
            fracs = jnp.where(here, rfrac[v, z], fracs)
    meta[1, 0:8] = offs
    meta[1, 8:16] = fracs

    peers = n_view + 1 - (slab == 0).astype(jnp.int32) - (slab == n_slab - 1).astype(jnp.int32)
    pl.semaphore_wait(barrier, peers)

    def send_lines(k, _):
        ag_copy(k).start()
        return 0

    lax.fori_loop(1, n_view, send_lines, 0)
    for side, has in sides:
        @pl.when(has)
        def _():
            meta_copy(side).start()

        @pl.when(jnp.logical_not(has))
        def _():
            slot = 0 if side == 0 else 2
            meta[slot] = jnp.zeros(meta.shape[1:], F32)
            sheared[slot] = jnp.zeros(sheared.shape[1:], BF16)
            img_in[side] = jnp.zeros(img_in.shape[1:], BF16)

    delta = lax.broadcasted_iota(jnp.int32, (2 * LANES, LANES), 0) - lax.broadcasted_iota(
        jnp.int32, (2 * LANES, LANES), 1
    )

    def place(s):
        whole = lax.shift_right_arithmetic(s, 7)
        return whole, s - whole * LANES

    def taps(s, first, second):
        _, r = place(s)
        return jnp.where(delta == r, first, jnp.where(delta == r + 1, second, 0.0)).astype(BF16)

    def build(y, _):
        for v in range(views):
            s = shift[me * views + v, y]
            f = frac[me * views + v, y]
            taps_f[v * n_lines + y] = taps(s, 1.0 - f, f)
            taps_b[v * n_lines + y] = taps(-s - 1, f, 1.0 - f)
        return 0

    lax.fori_loop(0, n_lines, build, 0)

    def put(ref, at, low, high):
        zeros = jnp.zeros((z_dev, margin), F32)
        top = jnp.concatenate([zeros, low, high[:, :margin]], axis=1)
        bottom = jnp.concatenate([low[:, half - margin :], high, zeros], axis=1)
        both = jnp.concatenate([top, bottom], axis=0).astype(BF16)
        for b in range(both.shape[1] // LANES):
            ref[at, b] = both[:, b * LANES : (b + 1) * LANES]

    def windows(ref, at, s):
        whole, _ = place(s)
        taken = ref[at, pl.ds(margin // LANES + whole, blocks + 1)]
        taken = taken.reshape((blocks + 1) * 16, LANES)
        return jnp.concatenate([taken[:-16], taken[16:]], axis=1)

    acc[...] = jnp.zeros(acc.shape, F32)

    def project(k, _):
        src = lax.rem(me + k, n_view)

        @pl.when(k > 0)
        def _():
            ag_arrival(src).wait_recv()

        for l in range(2):
            y = 2 * src + l
            x = gat[src].astype(F32)[l * z_dev : (l + 1) * z_dev]
            put(lines, y, x[:, :half], x[:, half:])
            for v in range(views):
                s = shift[me * views + v, y]
                acc[v] += dot(windows(lines, y, s), taps_f[v * n_lines + y])
        return 0

    lax.fori_loop(0, n_view, project, 0)
    for v in range(views):
        for b in range(blocks):
            sheared[1, 16 * v : 16 * (v + 1), b * LANES : (b + 1) * LANES] = acc[
                v, 16 * b : 16 * (b + 1)
            ].astype(BF16)

    for side, has in sides:
        @pl.when(has)
        def _():
            sheared_copy(side).start()

    rows = 2 * views * row_dev
    row = lax.broadcasted_iota(jnp.int32, (rows, LANES), 0)
    col = lax.broadcasted_iota(jnp.int32, (rows, LANES), 1)
    same = ((row // (views * row_dev)) == (col // 8) % 2) & ((row // row_dev) % views == col // 16)
    above_slice = (row % row_dev - (col % 8) * row_dev // z_dev).astype(F32)

    def weights(slot):
        past = above_slice - (meta[slot, 0:1] + float((slot - 1) * row_dev)) - meta[slot, 8:9]
        return jnp.where(same, jnp.maximum(1.0 - jnp.abs(past), 0.0), 0.0)

    for side, has in sides:
        @pl.when(has)
        def _():
            meta_copy(1 - side).wait_recv()

    keep = 2 * views * z_dev
    own = weights(1)
    below = weights(0)
    above = weights(2)
    proj = dot(own[:, :keep].astype(BF16), sheared[1])
    for side, has in sides:
        @pl.when(has)
        def _():
            sheared_copy(1 - side).wait_recv()
    proj += dot(below[:, :keep].astype(BF16), sheared[0])
    proj += dot(above[:, :keep].astype(BF16), sheared[2])

    for h in range(2):
        for v in range(views):
            at = slice(h * half, (h + 1) * half)
            lo = (h * views + v) * row_dev
            value = (ray[v, :, at] * (meas[v, :, at] - proj[lo : lo + row_dev])).astype(BF16)
            res[v, :, at] = value
            resid[lo : lo + row_dev] = value

    img_out[0] = dot(below.T[:keep].astype(BF16), resid[...]).astype(BF16)
    img_out[1] = dot(above.T[:keep].astype(BF16), resid[...]).astype(BF16)
    for side, has in sides:
        @pl.when(has)
        def _():
            image_copy(side).start()
    mine = dot(own.T[:keep].astype(BF16), resid[...])
    for side, has in sides:
        @pl.when(has)
        def _():
            image_copy(1 - side).wait_recv()
    mine += img_in[0].astype(F32) + img_in[1].astype(F32)
    for v in range(views):
        put(images, v, mine[16 * v : 16 * v + 8], mine[16 * v + 8 : 16 * v + 16])

    def spread(k, _):
        dest = lax.rem(me + k, n_view)
        for l in range(2):
            y = 2 * dest + l
            total = jnp.zeros((blocks * 16, LANES), F32)
            for v in range(views):
                s = -shift[me * views + v, y] - 1
                total += dot(windows(images, v, s), taps_b[v * n_lines + y])
            total = total.astype(BF16)
            for b in range(blocks):
                back_out[dest, 16 * l : 16 * (l + 1), b * LANES : (b + 1) * LANES] = total[
                    16 * b : 16 * (b + 1)
                ]

        @pl.when(k < n_view)
        def _():
            rs_copy(k).start()

        return 0

    lax.fori_loop(1, n_view + 1, spread, 0)

    for l in range(2):
        for h in range(2):
            at = slice(h * half, (h + 1) * half)
            rows_at = slice(16 * l + 8 * h, 16 * l + 8 * h + 8)
            acc_at = back_out[me, 16 * l : 16 * l + 16].astype(F32)[8 * h : 8 * h + 8]
            upd[l, :, at] = acc_at

    def collect(k, _):
        src = lax.rem(me + k, n_view)
        rs_arrival(src).wait_recv()
        for l in range(2):
            part = back_in[src, 16 * l : 16 * l + 16].astype(F32)
            for h in range(2):
                at = slice(h * half, (h + 1) * half)
                upd[l, :, at] += part[8 * h : 8 * h + 8]
        return 0

    lax.fori_loop(1, n_view, collect, 0)
    upd[...] = vol[...] + vox[...] * upd[...]

    def drain(k, _):
        ag_copy(k).wait_send()
        rs_copy(k).wait_send()
        return 0

    lax.fori_loop(1, n_view, drain, 0)
    for side, has in sides:
        @pl.when(has)
        def _():
            meta_copy(side).wait_send()
            sheared_copy(side).wait_send()
            image_copy(side).wait_send()


def per_device(volume, vox_inv, measured, ray_inv, col_shift, col_frac, row_offset, row_frac):
    y_dev, z_dev, width = volume.shape
    row_dev, views = measured.shape[:2]
    n_view, n_slab = lax.axis_size("view"), lax.axis_size("slab")
    half = width // 2
    margin = (width // 8 // LANES + 1) * LANES
    n_lines = n_view * y_dev
    packed = 2 * views * z_dev
    vmem = pl.BlockSpec(memory_space=pltpu.VMEM)
    smem = pl.BlockSpec(memory_space=pltpu.SMEM)
    dma = pltpu.SemaphoreType.DMA
    sizes = (n_view, n_slab, views, z_dev, row_dev, width)
    upd, res = pl.pallas_call(
        functools.partial(kernel, sizes),
        out_shape=[
            jax.ShapeDtypeStruct(volume.shape, F32),
            jax.ShapeDtypeStruct((views, row_dev, width), BF16),
        ],
        in_specs=[vmem] * 4 + [smem] * 4,
        out_specs=[vmem] * 2,
        scratch_shapes=[
            pltpu.VMEM((n_view, y_dev * z_dev, width), BF16),
            pltpu.VMEM((n_lines, (half + 2 * margin) // LANES, 2 * z_dev, LANES), BF16),
            pltpu.VMEM((views * n_lines, 2 * LANES, LANES), BF16),
            pltpu.VMEM((views * n_lines, 2 * LANES, LANES), BF16),
            pltpu.VMEM((views, half // LANES * 16, LANES), F32),
            pltpu.VMEM((3, packed, half), BF16),
            pltpu.VMEM((3, 16, LANES), F32),
            pltpu.VMEM((2 * views * row_dev, half), BF16),
            pltpu.VMEM((2, packed, half), BF16),
            pltpu.VMEM((2, packed, half), BF16),
            pltpu.VMEM((views, (half + 2 * margin) // LANES, 2 * z_dev, LANES), BF16),
            pltpu.VMEM((n_view, 2 * y_dev * z_dev, half), BF16),
            pltpu.VMEM((n_view, 2 * y_dev * z_dev, half), BF16),
            dma((n_view,)), dma((n_view,)),
            dma((2,)), dma((2,)),
            dma((2,)), dma((2,)),
            dma((2,)), dma((2,)),
            dma((n_view,)), dma((n_view,)),
        ],
        compiler_params=pltpu.CompilerParams(
            collective_id=0, has_side_effects=True, vmem_limit_bytes=48 * 1024 * 1024
        ),
    )(
        volume, vox_inv, measured.transpose(1, 0, 2), ray_inv.transpose(1, 0, 2),
        col_shift, col_frac, row_offset, row_frac,
    )
    return upd, res.transpose(1, 0, 2)


def solution(mesh):
    in_specs = (
        P("view", "slab", None),
        P("view", "slab", None),
        P("slab", "view", None),
        P("slab", "view", None),
        P(),
        P(),
        P("view", "slab"),
        P("view", "slab"),
    )
    out_specs = (P("view", "slab", None), P("slab", "view", None))
    return jax.shard_map(
        per_device, mesh=mesh, in_specs=in_specs, out_specs=out_specs, check_vma=False
    )
```

time: 256 us -> 49.2 us (0.19)
  the two profiles are of different devices: /device:TPU:0 before, /device:TPU:11 now
where the time goes in v1:
time: 49.2 us; the launch traced here: 48.3 us
  Pallas kernels  40.5 us (82%)
  local copies, waits for them, and re-layouts  7.09 us (14%)
  between operations  0.65 us (1%)
    pallas_call x1, Pallas kernels, per_device(): pl.pallas_call(functools.partial(kernel, sizes), out_shape=[jax.ShapeDtyp...  40.5 us
    unnamed x18, local copies, waits for them, and re-layouts  7.09 us

profile of v1, /device:TPU:11, one launch (start us, length us, event | category | flops | bytes accessed | tf_op | source)
XLA Modules:
  0.0 48.3 jit_solution(17607401298459863452)
XLA Ops:
  0.6 0.0 copy-start.6
  0.6 0.8 %copy.10.shift = s32[12,8]{1,0:T(8,128)S(1)} copy(s32[12,8]{0,1:T(8,128)} %param.12) | data formatting | bytes 768 | tf_op args[4]
  1.4 0.0 copy-done.6
  1.4 0.0 copy-start.4
  1.4 0.0 copy-start.5
  1.4 0.1 copy.11.frac
  1.5 0.6 %copy-done.4 = s32[3,8]{1,0:T(4,128)S(1)} copy-done((s32[3,8]{1,0:T(4,128)S(1)}, s32[3,8]{1,0:T(4,128)}, u32[]{:S(2)}) %copy-start.4) | copy-done | bytes 120
  2.1 0.0 copy-done.5
  2.1 0.0 copy-start
  2.1 1.1 %copy-done = f32[16,3,4096]{2,0,1:T(8,128)S(1)} copy-done((f32[16,3,4096]{2,0,1:T(8,128)S(1)}, f32[16,3,4096]{2,0,1:T(8,128)}, u32[]{:S(2)}) %copy-start) | copy-done | bytes 786456
  3.2 0.0 copy-start.1
  3.3 1.1 %copy-done.1 = f32[16,3,4096]{2,0,1:T(8,128)S(1)} copy-done((f32[16,3,4096]{2,0,1:T(8,128)S(1)}, f32[16,3,4096]{2,0,1:T(8,128)}, u32[]{:S(2)}) %copy-start.1) | copy-done | bytes 786456
  4.4 0.0 copy-start.2
  4.4 0.9 %copy-done.2 = f32[2,8,4096]{2,1,0:T(8,128)S(1)} copy-done((f32[2,8,4096]{2,1,0:T(8,128)S(1)}, f32[2,8,4096]{2,1,0:T(8,128)}, u32[]{:S(2)}) %copy-start.2) | copy-done | bytes 262168
  5.3 0.0 copy-start.3
  5.3 0.9 %copy-done.3 = f32[2,8,4096]{2,1,0:T(8,128)S(1)} copy-done((f32[2,8,4096]{2,1,0:T(8,128)S(1)}, f32[2,8,4096]{2,1,0:T(8,128)}, u32[]{:S(2)}) %copy-start.3) | copy-done | bytes 262168
  6.3 40.5 %shard_map.95 = (f32[2,8,4096]{2,1,0:T(8,128)S(1)}, bf16[3,16,4096]{2,1,0:T(8,128)(2,1)S(1)}) custom-call(f32[2,8,4096]{2,1,0:T(8,128)S(1)} %copy-done.2, f32[2,8,4096]{2,1,0:T(8,128)S(1)} %copy-done.3, f32[3,16,4096]{2,1,0:T(8,128)S(1)} %bitcast.3, f32[3,16,4096]{2,1,0:T(8,128)S(1)} %bitcast.4, s32[12,8]{1,0:T(8,128)S(1)} %copy.10.shift, ...), custom_call_target="tpu_custom_call" | custom-call | tf_op jit(solution)/shard_map/pallas_call | solution.py:303
  46.8 0.7 %copy.14 = f32[2,8,4096]{2,1,0:T(8,128)} copy(f32[2,8,4096]{2,1,0:T(8,128)S(1)} %get-tuple-element.8) | data formatting | bytes 524288
  47.5 0.7 %copy.15 = bf16[16,3,4096]{2,0,1:T(8,128)(2,1)} copy(bf16[16,3,4096]{2,0,1:T(8,128)(2,1)S(1)} %bitcast.5) | data formatting | bytes 786432
Async XLA Ops:
  0.6 0.8 %copy-start.6 = (f32[12,8]{0,1:T(8,128)S(1)}, f32[12,8]{0,1:T(8,128)}, u32[]{:S(2)}) copy-start(f32[12,8]{0,1:T(8,128)} %param.13) | copy-start | bytes 1156
  1.4 0.7 %copy-start.4 = (s32[3,8]{1,0:T(4,128)S(1)}, s32[3,8]{1,0:T(4,128)}, u32[]{:S(2)}) copy-start(s32[3,8]{1,0:T(4,128)} %off.1) | copy-start | bytes 292
  1.4 0.7 %copy-start.5 = (f32[3,8]{1,0:T(4,128)S(1)}, f32[3,8]{1,0:T(4,128)}, u32[]{:S(2)}) copy-start(f32[3,8]{1,0:T(4,128)} %rfrac.1) | copy-start | bytes 292
  2.1 1.1 %copy-start = (f32[16,3,4096]{2,0,1:T(8,128)S(1)}, f32[16,3,4096]{2,0,1:T(8,128)}, u32[]{:S(2)}) copy-start(f32[16,3,4096]{2,0,1:T(8,128)} %param.10) | copy-start | bytes 2359300
  3.2 1.1 %copy-start.1 = (f32[16,3,4096]{2,0,1:T(8,128)S(1)}, f32[16,3,4096]{2,0,1:T(8,128)}, u32[]{:S(2)}) copy-start(f32[16,3,4096]{2,0,1:T(8,128)} %param.11) | copy-start | bytes 2359300
  4.4 0.9 %copy-start.2 = (f32[2,8,4096]{2,1,0:T(8,128)S(1)}, f32[2,8,4096]{2,1,0:T(8,128)}, u32[]{:S(2)}) copy-start(f32[2,8,4096]{2,1,0:T(8,128)} %vol.1) | copy-start | bytes 786436
  5.3 0.9 %copy-start.3 = (f32[2,8,4096]{2,1,0:T(8,128)S(1)}, f32[2,8,4096]{2,1,0:T(8,128)}, u32[]{:S(2)}) copy-start(f32[2,8,4096]{2,1,0:T(8,128)} %vox.1) | copy-start | bytes 786436

commit v2 on v1

--- a/solution.py
+++ b/solution.py
@@ -17,20 +17,28 @@
 
 
 def kernel(
-    sizes, vol, vox, meas, ray, shift, frac, off, rfrac, upd, res,
-    gat, lines, taps_f, taps_b, acc, sheared, meta, resid, img_out, img_in, images, back_out, back_in,
-    ag_send, ag_recv, me_send, me_recv, sh_send, sh_recv, im_send, im_recv, rs_send, rs_recv,
+    sizes, vol_at, vox_at, meas_at, ray_at, shift, frac, off, rfrac, upd, res,
+    vol, vox, meas, ray,
+    gat, lines, taps_f, taps_b, acc, sheared, sheared_out, sheared_in, meta, resid, img_out, img_in, images, back_out, back_in,
+    ag_send, ag_recv, me_send, me_recv, sh_send, sh_recv, im_send, im_recv, rs_send, rs_recv, load_sem,
 ):
     n_view, n_slab, views, z_dev, row_dev, width = sizes
     half = width // 2
     margin = (lines.shape[1] * LANES - half) // 2
     blocks = half // LANES
+    quarter = half // 2
     n_lines = 2 * n_view
     me = lax.axis_index("view")
     slab = lax.axis_index("slab")
     has_lo = slab > 0
     has_hi = slab < n_slab - 1
 
+    loads = [
+        pltpu.make_async_copy(src, dst, load_sem.at[i])
+        for i, (src, dst) in enumerate(((vol_at, vol), (meas_at, meas), (ray_at, ray), (vox_at, vox)))
+    ]
+    loads[0].start()
+
     def ag_copy(k):
         dest = lax.rem(me + k, n_view)
         return pltpu.make_async_remote_copy(
@@ -63,10 +71,10 @@
     sides = ((0, has_lo), (1, has_hi))
 
     def meta_copy(side):
-        return halo(meta.at[1], meta, me_send, me_recv, side, 0, 2)
+        return halo(meta.at[3 + side], meta, me_send, me_recv, side, 0, 2)
 
     def sheared_copy(side):
-        return halo(sheared.at[1], sheared, sh_send, sh_recv, side, 0, 2)
+        return halo(sheared_out.at[side], sheared_in, sh_send, sh_recv, side, 0, 1)
 
     def image_copy(side):
         return halo(img_out.at[side], img_in, im_send, im_recv, side, 0, 1)
@@ -83,18 +91,22 @@
         def _():
             pl.semaphore_signal(barrier, inc=1, device_id={"slab": slab - 1 if side == 0 else slab + 1})
 
+    loads[0].wait()
     gat[me] = vol[...].reshape(2 * z_dev, width).astype(BF16)
 
     lane = lax.broadcasted_iota(jnp.int32, (8, LANES), 1)
-    offs = jnp.zeros((8, LANES), F32)
-    fracs = jnp.zeros((8, LANES), F32)
-    for v in range(views):
-        for z in range(z_dev):
-            here = (lane // 16 == v) & (lane % 8 == z)
-            offs = jnp.where(here, off[v, z].astype(F32), offs)
-            fracs = jnp.where(here, rfrac[v, z], fracs)
-    meta[1, 0:8] = offs
-    meta[1, 8:16] = fracs
+    few = z_dev // 2
+    slice_of = {1: lane % z_dev, 3: lane % few, 4: lane % few + few}
+    for slot, slices in slice_of.items():
+        offs = jnp.zeros((8, LANES), F32)
+        fracs = jnp.zeros((8, LANES), F32)
+        for v in range(views):
+            for z in range(z_dev):
+                here = (lane // 16 == v) & (slices == z)
+                offs = jnp.where(here, off[v, z].astype(F32), offs)
+                fracs = jnp.where(here, rfrac[v, z], fracs)
+        meta[slot, 0:8] = offs
+        meta[slot, 8:16] = fracs
 
     peers = n_view + 1 - (slab == 0).astype(jnp.int32) - (slab == n_slab - 1).astype(jnp.int32)
     pl.semaphore_wait(barrier, peers)
@@ -104,6 +116,8 @@
         return 0
 
     lax.fori_loop(1, n_view, send_lines, 0)
+    for load in loads[1:]:
+        load.start()
     for side, has in sides:
         @pl.when(has)
         def _():
@@ -113,7 +127,7 @@
         def _():
             slot = 0 if side == 0 else 2
             meta[slot] = jnp.zeros(meta.shape[1:], F32)
-            sheared[slot] = jnp.zeros(sheared.shape[1:], BF16)
+            sheared_in[side] = jnp.zeros(sheared_in.shape[1:], BF16)
             img_in[side] = jnp.zeros(img_in.shape[1:], BF16)
 
     delta = lax.broadcasted_iota(jnp.int32, (2 * LANES, LANES), 0) - lax.broadcasted_iota(
@@ -130,8 +144,8 @@
 
     def build(y, _):
         for v in range(views):
-            s = shift[me * views + v, y]
-            f = frac[me * views + v, y]
+            s = shift[y, me * views + v]
+            f = frac[y, me * views + v]
             taps_f[v * n_lines + y] = taps(s, 1.0 - f, f)
             taps_b[v * n_lines + y] = taps(-s - 1, f, 1.0 - f)
         return 0
@@ -166,71 +180,117 @@
             x = gat[src].astype(F32)[l * z_dev : (l + 1) * z_dev]
             put(lines, y, x[:, :half], x[:, half:])
             for v in range(views):
-                s = shift[me * views + v, y]
+                s = shift[y, me * views + v]
                 acc[v] += dot(windows(lines, y, s), taps_f[v * n_lines + y])
         return 0
 
     lax.fori_loop(0, n_view, project, 0)
+    low_rows = lax.broadcasted_iota(jnp.int32, (z_dev, LANES), 0) < few
+
+    def turn(x):
+        return pltpu.roll(x, few, 0)
+
+    for v in range(views):
+        for b in range(blocks // 2):
+            first = acc[v, 16 * b : 16 * (b + 1)]
+            second = acc[v, 16 * (b + blocks // 2) : 16 * (b + blocks // 2 + 1)]
+            down, up = [], []
+            for h in range(2):
+                x, y = first[8 * h : 8 * h + 8], second[8 * h : 8 * h + 8]
+                down.append(jnp.where(low_rows, x, turn(y)))
+                up.append(jnp.where(low_rows, turn(x), y))
+            at = (slice(16 * v, 16 * (v + 1)), slice(b * LANES, (b + 1) * LANES))
+            sheared_out[(0,) + at] = jnp.concatenate(down, axis=0).astype(BF16)
+            sheared_out[(1,) + at] = jnp.concatenate(up, axis=0).astype(BF16)
+
+    for side, has in sides:
+        @pl.when(has)
+        def _():
+            sheared_copy(side).start()
+
     for v in range(views):
         for b in range(blocks):
-            sheared[1, 16 * v : 16 * (v + 1), b * LANES : (b + 1) * LANES] = acc[
+            sheared[16 * v : 16 * (v + 1), b * LANES : (b + 1) * LANES] = acc[
                 v, 16 * b : 16 * (b + 1)
             ].astype(BF16)
 
-    for side, has in sides:
-        @pl.when(has)
-        def _():
-            sheared_copy(side).start()
-
-    rows = 2 * views * row_dev
-    row = lax.broadcasted_iota(jnp.int32, (rows, LANES), 0)
-    col = lax.broadcasted_iota(jnp.int32, (rows, LANES), 1)
-    same = ((row // (views * row_dev)) == (col // 8) % 2) & ((row // row_dev) % views == col // 16)
-    above_slice = (row % row_dev - (col % 8) * row_dev // z_dev).astype(F32)
-
-    def weights(slot):
-        past = above_slice - (meta[slot, 0:1] + float((slot - 1) * row_dev)) - meta[slot, 8:9]
-        return jnp.where(same, jnp.maximum(1.0 - jnp.abs(past), 0.0), 0.0)
+    span = 2 * views * row_dev
+
+    def grid_of(count):
+        shape = (count * span, LANES)
+        row = lax.broadcasted_iota(jnp.int32, shape, 0)
+        col = lax.broadcasted_iota(jnp.int32, shape, 1)
+        here = ((row // row_dev) % views == col // 16) & (
+            (row // (views * row_dev)) % 2 == (col // 8) % 2
+        )
+        return row, col, here
+
+    def weights(slot, row, slices, here):
+        rows_past = (row % row_dev - slices * row_dev // z_dev).astype(F32)
+        past = rows_past - (meta[slot, 0:1] + float((slot - 1) * row_dev)) - meta[slot, 8:9]
+        return jnp.where(here, jnp.maximum(1.0 - jnp.abs(past), 0.0), 0.0)
+
+    keep = 2 * views * z_dev
+    row, col, here = grid_of(1)
+    own = weights(1, row, col % z_dev, here)
+    proj = dot(own[:, :keep].astype(BF16), sheared[...])
 
     for side, has in sides:
         @pl.when(has)
         def _():
             meta_copy(1 - side).wait_recv()
 
-    keep = 2 * views * z_dev
-    own = weights(1)
-    below = weights(0)
-    above = weights(2)
-    proj = dot(own[:, :keep].astype(BF16), sheared[1])
+    row, col, here = grid_of(2)
+    here = here & (row // span == (col // few) % 2)
+    below = weights(0, row, col % few + few, here)
+    above = weights(2, row, col % few, here)
+    below_t = below.T[:keep].astype(BF16)
+    above_t = above.T[:keep].astype(BF16)
+    own_t = own.T[:keep].astype(BF16)
     for side, has in sides:
         @pl.when(has)
         def _():
             sheared_copy(1 - side).wait_recv()
-    proj += dot(below[:, :keep].astype(BF16), sheared[0])
-    proj += dot(above[:, :keep].astype(BF16), sheared[2])
-
+    beside = dot(below[:, :keep].astype(BF16), sheared_in[0])
+    beside += dot(above[:, :keep].astype(BF16), sheared_in[1])
+
+    loads[1].wait()
+    loads[2].wait()
     for h in range(2):
         for v in range(views):
             at = slice(h * half, (h + 1) * half)
             lo = (h * views + v) * row_dev
-            value = (ray[v, :, at] * (meas[v, :, at] - proj[lo : lo + row_dev])).astype(BF16)
+            here = proj[lo : lo + row_dev] + jnp.concatenate(
+                [beside[lo : lo + row_dev], beside[span + lo : span + lo + row_dev]], axis=1
+            )
+            value = (ray[v, :, at] * (meas[v, :, at] - here)).astype(BF16)
             res[v, :, at] = value
-            resid[lo : lo + row_dev] = value
-
-    img_out[0] = dot(below.T[:keep].astype(BF16), resid[...]).astype(BF16)
-    img_out[1] = dot(above.T[:keep].astype(BF16), resid[...]).astype(BF16)
+            resid[lo : lo + row_dev] = value[:, :quarter]
+            resid[span + lo : span + lo + row_dev] = value[:, quarter:]
+
+    img_out[0] = dot(below_t, resid[...]).astype(BF16)
+    img_out[1] = dot(above_t, resid[...]).astype(BF16)
     for side, has in sides:
         @pl.when(has)
         def _():
             image_copy(side).start()
-    mine = dot(own.T[:keep].astype(BF16), resid[...])
+    mine = jnp.concatenate([dot(own_t, resid[:span]), dot(own_t, resid[span:])], axis=1)
     for side, has in sides:
         @pl.when(has)
         def _():
             image_copy(1 - side).wait_recv()
-    mine += img_in[0].astype(F32) + img_in[1].astype(F32)
+    low_slices = lax.broadcasted_iota(jnp.int32, (z_dev, quarter), 0) < few
     for v in range(views):
-        put(images, v, mine[16 * v : 16 * v + 8], mine[16 * v + 8 : 16 * v + 16])
+        halves = []
+        under = img_in[0, 16 * v : 16 * (v + 1)].astype(F32)
+        over = img_in[1, 16 * v : 16 * (v + 1)].astype(F32)
+        for h in range(2):
+            x, y = under[8 * h : 8 * h + 8], over[8 * h : 8 * h + 8]
+            added = jnp.concatenate(
+                [jnp.where(low_slices, x, turn(y)), jnp.where(low_slices, turn(x), y)], axis=1
+            )
+            halves.append(mine[16 * v + 8 * h : 16 * v + 8 * h + 8] + added)
+        put(images, v, halves[0], halves[1])
 
     def spread(k, _):
         dest = lax.rem(me + k, n_view)
@@ -238,7 +298,7 @@
             y = 2 * dest + l
             total = jnp.zeros((blocks * 16, LANES), F32)
             for v in range(views):
-                s = -shift[me * views + v, y] - 1
+                s = -shift[y, me * views + v] - 1
                 total += dot(windows(images, v, s), taps_b[v * n_lines + y])
             total = total.astype(BF16)
             for b in range(blocks):
@@ -272,6 +332,7 @@
         return 0
 
     lax.fori_loop(1, n_view, collect, 0)
+    loads[3].wait()
     upd[...] = vol[...] + vox[...] * upd[...]
 
     def drain(k, _):
@@ -306,19 +367,25 @@
             jax.ShapeDtypeStruct(volume.shape, F32),
             jax.ShapeDtypeStruct((views, row_dev, width), BF16),
         ],
-        in_specs=[vmem] * 4 + [smem] * 4,
+        in_specs=[pl.BlockSpec(memory_space=pltpu.HBM)] * 4 + [smem] * 4,
         out_specs=[vmem] * 2,
         scratch_shapes=[
+            pltpu.VMEM(volume.shape, F32),
+            pltpu.VMEM(volume.shape, F32),
+            pltpu.VMEM((views, row_dev, width), F32),
+            pltpu.VMEM((views, row_dev, width), F32),
             pltpu.VMEM((n_view, y_dev * z_dev, width), BF16),
             pltpu.VMEM((n_lines, (half + 2 * margin) // LANES, 2 * z_dev, LANES), BF16),
             pltpu.VMEM((views * n_lines, 2 * LANES, LANES), BF16),
             pltpu.VMEM((views * n_lines, 2 * LANES, LANES), BF16),
             pltpu.VMEM((views, half // LANES * 16, LANES), F32),
-            pltpu.VMEM((3, packed, half), BF16),
-            pltpu.VMEM((3, 16, LANES), F32),
-            pltpu.VMEM((2 * views * row_dev, half), BF16),
-            pltpu.VMEM((2, packed, half), BF16),
-            pltpu.VMEM((2, packed, half), BF16),
+            pltpu.VMEM((packed, half), BF16),
+            pltpu.VMEM((2, packed, half // 2), BF16),
+            pltpu.VMEM((2, packed, half // 2), BF16),
+            pltpu.VMEM((5, 16, LANES), F32),
+            pltpu.VMEM((4 * views * row_dev, half // 2), BF16),
+            pltpu.VMEM((2, packed, half // 2), BF16),
+            pltpu.VMEM((2, packed, half // 2), BF16),
             pltpu.VMEM((views, (half + 2 * margin) // LANES, 2 * z_dev, LANES), BF16),
             pltpu.VMEM((n_view, 2 * y_dev * z_dev, half), BF16),
             pltpu.VMEM((n_view, 2 * y_dev * z_dev, half), BF16),
@@ -327,13 +394,14 @@
             dma((2,)), dma((2,)),
             dma((2,)), dma((2,)),
             dma((n_view,)), dma((n_view,)),
+            dma((4,)),
         ],
         compiler_params=pltpu.CompilerParams(
-            collective_id=0, has_side_effects=True, vmem_limit_bytes=48 * 1024 * 1024
+            collective_id=0, has_side_effects=True, vmem_limit_bytes=63 * 1024 * 1024
         ),
     )(
         volume, vox_inv, measured.transpose(1, 0, 2), ray_inv.transpose(1, 0, 2),
-        col_shift, col_frac, row_offset, row_frac,
+        col_shift.T, col_frac.T, row_offset, row_frac,
     )
     return upd, res.transpose(1, 0, 2)
 

time: 49.2 us -> 42.5 us (0.86)
  local copies, waits for them, and re-layouts: 7.09 us -> 2.47 us
  Pallas kernels: 40.5 us -> 38.6 us
    unnamed x18 -> x4, local copies, waits for them, and re-layouts: 7.09 us -> 2.47 us
    pallas_call x1, Pallas kernels: 40.5 us -> 38.6 us  [per_device(): pl.pallas_call(functools.partial(kernel, sizes), out_shape=[jax.ShapeDtyp...]
where the time goes in v2:
time: 42.5 us; the launch traced here: 41.7 us
  Pallas kernels  38.6 us (91%)
  local copies, waits for them, and re-layouts  2.47 us (6%)
  between operations  0.65 us (2%)
    pallas_call x1, Pallas kernels, per_device(): pl.pallas_call(functools.partial(kernel, sizes), out_shape=[jax.ShapeDtyp...  38.6 us
    unnamed x4, local copies, waits for them, and re-layouts  2.47 us

profile of v2, /device:TPU:11, one launch (start us, length us, event | category | flops | bytes accessed | tf_op | source)
XLA Modules:
  0.0 41.7 jit_solution(13463393907464318514)
XLA Ops:
  0.6 38.6 %shard_map.95 = (f32[2,8,4096]{2,1,0:T(8,128)}, bf16[3,16,4096]{2,1,0:T(8,128)(2,1)}) custom-call(f32[2,8,4096]{2,1,0:T(8,128)} %vol_at.1, f32[2,8,4096]{2,1,0:T(8,128)} %vox_at.1, f32[3,16,4096]{2,1,0:T(8,128)} %bitcast.5, f32[3,16,4096]{2,1,0:T(8,128)} %bitcast.6, s32[8,12]{1,0:T(8,128)} %bitcast.8, f32[8,12]{1,0:T(8,128)} %bitcast.9, s32[3,8]{1,0:T(4,128)} %off.1, ...), custom_call_target="tpu_custom_call" | custom-call | tf_op jit(solution)/shard_map/pallas_call | solution.py:364
  39.2 0.0 copy-start
  39.2 1.7 %copy.12 = f32[2,8,4096]{2,1,0:T(8,128)} copy(f32[2,8,4096]{2,1,0:T(8,128)} %get-tuple-element.8) | data formatting | bytes 524288
  40.9 0.0 copy-done
  40.9 0.7 %copy.13 = bf16[16,3,4096]{2,0,1:T(8,128)(2,1)} copy(bf16[16,3,4096]{2,0,1:T(8,128)(2,1)S(1)} %bitcast.7) | data formatting | bytes 786432
Async XLA Ops:
  39.2 1.7 %copy-start = (bf16[3,16,4096]{2,1,0:T(8,128)(2,1)S(1)}, bf16[3,16,4096]{2,1,0:T(8,128)(2,1)}, u32[]{:S(2)}) copy-start(bf16[3,16,4096]{2,1,0:T(8,128)(2,1)} %get-tuple-element.5) | copy-start | bytes 1179652

commit v3 on v2

--- a/solution.py
+++ b/solution.py
@@ -39,19 +39,33 @@
     ]
     loads[0].start()
 
+    def peer(k):
+        return lax.rem(jnp.where(2 * me < n_view, me + k, me + n_view - k), n_view)
+
+    inner = (me > 0) & (me < n_view - 1) & (n_view == 4)
+
+    def handed_on(k):
+        return inner & (k == 2)
+
     def ag_copy(k):
-        dest = lax.rem(me + k, n_view)
+        dest = peer(k)
         return pltpu.make_async_remote_copy(
             gat.at[me], gat.at[me], ag_send.at[k], ag_recv.at[me], device_id={"view": dest}
         )
 
+    def ag_forward():
+        src = peer(1)
+        return pltpu.make_async_remote_copy(
+            gat.at[src], gat.at[src], ag_send.at[0], ag_recv.at[src], device_id={"view": 2 * me - src}
+        )
+
     def ag_arrival(src):
         return pltpu.make_async_remote_copy(
             gat.at[src], gat.at[src], ag_send.at[0], ag_recv.at[src], device_id={"view": src}
         )
 
     def rs_copy(k):
-        dest = lax.rem(me + k, n_view)
+        dest = peer(k)
         return pltpu.make_async_remote_copy(
             back_out.at[dest], back_in.at[me], rs_send.at[k], rs_recv.at[me], device_id={"view": dest}
         )
@@ -112,7 +126,10 @@
     pl.semaphore_wait(barrier, peers)
 
     def send_lines(k, _):
-        ag_copy(k).start()
+        @pl.when(jnp.logical_not(handed_on(k)))
+        def _():
+            ag_copy(k).start()
+
         return 0
 
     lax.fori_loop(1, n_view, send_lines, 0)
@@ -169,11 +186,15 @@
     acc[...] = jnp.zeros(acc.shape, F32)
 
     def project(k, _):
-        src = lax.rem(me + k, n_view)
+        src = peer(k)
 
         @pl.when(k > 0)
         def _():
             ag_arrival(src).wait_recv()
+
+        @pl.when(inner & (k == 1))
+        def _():
+            ag_forward().start()
 
         for l in range(2):
             y = 2 * src + l
@@ -292,8 +313,9 @@
             halves.append(mine[16 * v + 8 * h : 16 * v + 8 * h + 8] + added)
         put(images, v, halves[0], halves[1])
 
-    def spread(k, _):
-        dest = lax.rem(me + k, n_view)
+    def spread(i, _):
+        k = n_view - i
+        dest = peer(k)
         for l in range(2):
             y = 2 * dest + l
             total = jnp.zeros((blocks * 16, LANES), F32)
@@ -306,7 +328,7 @@
                     16 * b : 16 * (b + 1)
                 ]
 
-        @pl.when(k < n_view)
+        @pl.when(k > 0)
         def _():
             rs_copy(k).start()
 
@@ -322,7 +344,7 @@
             upd[l, :, at] = acc_at
 
     def collect(k, _):
-        src = lax.rem(me + k, n_view)
+        src = peer(k)
         rs_arrival(src).wait_recv()
         for l in range(2):
             part = back_in[src, 16 * l : 16 * l + 16].astype(F32)
@@ -336,11 +358,19 @@
     upd[...] = vol[...] + vox[...] * upd[...]
 
     def drain(k, _):
-        ag_copy(k).wait_send()
+        @pl.when(jnp.logical_not(handed_on(k)))
+        def _():
+            ag_copy(k).wait_send()
+
         rs_copy(k).wait_send()
         return 0
 
     lax.fori_loop(1, n_view, drain, 0)
+
+    @pl.when(inner)
+    def _():
+        ag_forward().wait_send()
+
     for side, has in sides:
         @pl.when(has)
         def _():

time: 42.5 us -> 38.7 us (0.911); the launches traced: 41.7 us -> 38.5 us
  Pallas kernels: 38.6 us -> 35.4 us
    pallas_call x1, Pallas kernels: 38.6 us -> 35.4 us  [per_device(): pl.pallas_call(functools.partial(kernel, sizes), out_shape=[jax.ShapeDtyp...]
where the time goes in v3:
time: 38.7 us; the launch traced here: 38.5 us
  Pallas kernels  35.4 us (91%)
  local copies, waits for them, and re-layouts  2.47 us (6%)
  between operations  0.65 us (2%)
    pallas_call x1, Pallas kernels, per_device(): pl.pallas_call(functools.partial(kernel, sizes), out_shape=[jax.ShapeDtyp...  35.4 us
    unnamed x4, local copies, waits for them, and re-layouts  2.47 us

profile of v3, /device:TPU:11, one launch (start us, length us, event | category | flops | bytes accessed | tf_op | source)
XLA Modules:
  0.0 38.5 jit_solution(14684002122074614019)
XLA Ops:
  0.6 35.4 %shard_map.95 = (f32[2,8,4096]{2,1,0:T(8,128)}, bf16[3,16,4096]{2,1,0:T(8,128)(2,1)}) custom-call(f32[2,8,4096]{2,1,0:T(8,128)} %vol_at.1, f32[2,8,4096]{2,1,0:T(8,128)} %vox_at.1, f32[3,16,4096]{2,1,0:T(8,128)} %bitcast.5, f32[3,16,4096]{2,1,0:T(8,128)} %bitcast.6, s32[8,12]{1,0:T(8,128)} %bitcast.8, f32[8,12]{1,0:T(8,128)} %bitcast.9, s32[3,8]{1,0:T(4,128)} %off.1, ...), custom_call_target="tpu_custom_call" | custom-call | tf_op jit(solution)/shard_map/pallas_call | solution.py:394
  36.0 0.0 copy-start
  36.0 1.7 %copy.12 = f32[2,8,4096]{2,1,0:T(8,128)} copy(f32[2,8,4096]{2,1,0:T(8,128)} %get-tuple-element.8) | data formatting | bytes 524288
  37.7 0.0 copy-done
  37.7 0.7 %copy.13 = bf16[16,3,4096]{2,0,1:T(8,128)(2,1)} copy(bf16[16,3,4096]{2,0,1:T(8,128)(2,1)S(1)} %bitcast.7) | data formatting | bytes 786432
Async XLA Ops:
  36.0 1.7 %copy-start = (bf16[3,16,4096]{2,1,0:T(8,128)(2,1)S(1)}, bf16[3,16,4096]{2,1,0:T(8,128)(2,1)}, u32[]{:S(2)}) copy-start(bf16[3,16,4096]{2,1,0:T(8,128)(2,1)} %get-tuple-element.5) | copy-start | bytes 1179652
